TPU v7x, 256 devices: a whole 4x4x8 slice. The times are simulated.
256 devices in a mesh: col: 16 (over y, x), grp: 16 (over z, core).
Axes of the slice: x: 4, y: 4, z: 8, core: 2. Of those that a mesh axis runs over, the one named last changes fastest.
Arguments:
- table: float32 [256, 131072], P('col', 'grp'), may hold values from -6 to 6
- hot: float32 [256, 8192], P('col'), may hold values from -6 to 6
- accum: float32 [8192], replicated, may hold values from 0.05 to 0.5
- pending: float32 [16, 256, 8192], P('grp', 'col'), may hold values from -0.6 to 0.6
- slot_ids: int32 [2048], replicated, may hold values from 0 to 8191, as said below
- demote_ids: int32 [2048], replicated, may hold values from 0 to 131071, as said below
- promote_ids: int32 [2048], replicated, may hold values from 0 to 131071, as said below
- bag_rows: int32 [4, 8, 32768], P(None, None, 'grp'), may hold values from 0 to 8191
- bag_mask: int32 [4, 8, 32768], P(None, None, 'grp'), may hold values 0 or 1
- labels: int32 [16, 2048], P('col', 'grp'), may hold values 0 or 1
- cross_down: bfloat16 [2048, 512], replicated, may hold values from -0.125 to 0.125
- cross_up: bfloat16 [512, 2048], replicated, may hold values from -0.25 to 0.25
- cross_bias: float32 [2048], replicated, may hold values from -3 to 3
- top_weight: bfloat16 [2048, 1024], replicated, may hold values from -0.125 to 0.125
- top_bias: float32 [1024], replicated, may hold values from -3 to 3
- out_weight: bfloat16 [1024], replicated, may hold values from -0.1875 to 0.1875
Outputs:
- new_table: float32 [256, 131072], P('col', 'grp')
- new_hot: float32 [256, 8192], P('col')
- new_accum: float32 [8192], replicated
- logits: float32 [16, 2048], P('col', 'grp')
Inputs may be any that keep to these rules, and one draw needn't show every extreme that they name: `slot_ids`: distinct; includes 0 and 8191. `demote_ids`: distinct; includes 0 and 131071. `promote_ids`: distinct; includes 0 and 131071.
All inputs are finite; a program needn't handle non-finite values. No bound on the sum of `bag_mask` or of `labels` on one device may be relied on, other than what follows from the above.
Results may differ from a plain program's by a relative error of at most 0.006.
Values may be sent and summed in bfloat16 or wider, within the bound.
A program may use at most 192 MiB of HBM per device.

v0:
```python
import jax
import jax.numpy as jnp
from jax import lax
from jax.sharding import PartitionSpec as P

E = 256


step_size = 0.2
adagrad_eps = 1e-06


def dense_step(x0, label, cross_down, cross_up, cross_bias, top_weight, top_bias, out_weight):
    lowrank = jnp.dot(x0, cross_down, preferred_element_type=jnp.float32).astype(jnp.bfloat16)
    crossgate = jnp.dot(lowrank, cross_up, preferred_element_type=jnp.float32) + cross_bias
    x0_wide = x0.astype(jnp.float32)
    x1 = (x0_wide * crossgate + x0_wide).astype(jnp.bfloat16)
    preact = jnp.dot(x1, top_weight, preferred_element_type=jnp.float32) + top_bias
    sig = jax.nn.sigmoid(preact)
    hidden = (preact * sig).astype(jnp.bfloat16)
    logit = jnp.dot(hidden, out_weight, preferred_element_type=jnp.float32)
    dlogit = jax.nn.sigmoid(logit) - label.astype(jnp.float32)
    slope = sig * (1.0 + preact * (1.0 - sig))
    dhidden = (dlogit[:, None] * out_weight.astype(jnp.float32)[None, :] * slope).astype(
        jnp.bfloat16
    )
    dx1 = jnp.dot(dhidden, top_weight.T, preferred_element_type=jnp.float32)
    dgate = (dx1 * x0_wide).astype(jnp.bfloat16)
    dlow = jnp.dot(dgate, cross_up.T, preferred_element_type=jnp.float32).astype(jnp.bfloat16)
    dx0 = (
        dx1 * (crossgate + 1.0) + jnp.dot(dlow, cross_down.T, preferred_element_type=jnp.float32)
    ).astype(jnp.bfloat16)
    return (logit, dx0)


def per_device(
    table,
    hot,
    accum,
    pending,
    slot_ids,
    demote_ids,
    promote_ids,
    bag_rows,
    bag_mask,
    labels,
    cross_down,
    cross_up,
    cross_bias,
    top_weight,
    top_bias,
    out_weight,
):
    rows_dev = table.shape[1]
    width = hot.shape[0]
    slots = bag_rows.shape[0]
    first_row = lax.axis_index("grp") * rows_dev
    synced = hot + lax.psum(pending[0], "grp")
    demote_local = demote_ids - first_row
    demote_owned = (demote_local >= 0) & (demote_local < rows_dev)
    demote_target = jnp.where(demote_owned, demote_local, rows_dev)
    new_table = table.at[:, demote_target].set(synced[:, slot_ids], mode="drop")
    promote_local = promote_ids - first_row
    promote_owned = (promote_local >= 0) & (promote_local < rows_dev)
    picked = new_table[:, jnp.clip(promote_local, 0, rows_dev - 1)]
    fetched = jnp.where(promote_owned[None, :], picked, 0.0)
    arrived = lax.psum(fetched, "grp")
    refreshed = synced.at[:, slot_ids].set(arrived)
    weights = bag_mask.astype(jnp.float32)
    pooled = refreshed[:, bag_rows[0]] * weights[0][None]
    for slot in range(1, slots):
        pooled = pooled + refreshed[:, bag_rows[slot]] * weights[slot][None]
    pooled = pooled.astype(jnp.bfloat16)
    gathered = lax.all_to_all(pooled, "col", split_axis=2, concat_axis=0, tiled=True)
    samples = gathered.shape[2]
    x0 = gathered.transpose(2, 1, 0).reshape(samples, -1)
    logit, dx0 = dense_step(
        x0, labels[0], cross_down, cross_up, cross_bias, top_weight, top_bias, out_weight
    )
    back = dx0.reshape(samples, gathered.shape[1], gathered.shape[0]).transpose(2, 1, 0)
    returned = lax.all_to_all(back, "col", split_axis=0, concat_axis=2, tiled=True).astype(
        jnp.float32
    )
    partial_value = jnp.zeros(hot.shape, jnp.float32)
    for slot in range(slots):
        terms = returned * weights[slot][None]
        partial_value = partial_value.at[:, bag_rows[slot].reshape(-1)].add(
            terms.reshape(width, -1)
        )
    grad = lax.psum(partial_value.astype(jnp.bfloat16), "grp").astype(jnp.float32)
    squares = lax.psum(jnp.sum(grad * grad, axis=0), "col")
    new_accum = accum + squares / E
    new_hot = refreshed - step_size * grad / jnp.sqrt(new_accum + adagrad_eps)[None, :]
    return (new_table, new_hot, new_accum, logit[None, :])


def solution(mesh):
    return jax.shard_map(
        per_device,
        mesh=mesh,
        in_specs=(
            P("col", "grp"),
            P("col", None),
            P(),
            P("grp", "col", None),
            P(),
            P(),
            P(),
            P(None, None, "grp"),
            P(None, None, "grp"),
            P("col", "grp"),
            P(),
            P(),
            P(),
            P(),
            P(),
            P(),
        ),
        out_specs=(P("col", "grp"), P("col", None), P(), P("col", "grp")),
        check_vma=False,
    )
```

profile of v0, /device:TPU:1, one launch (start us, length us, event | category | flops | bytes accessed | tf_op | source)
XLA Modules:
  0.0 1173.6 jit_solution(4567532981456993598)
XLA Ops:
  7.2 3.7 copy.110
  11.1 0.7 slice_bitcast_fusion.8
  11.7 0.7 fusion.25
  13.0 0.9 copy.143
  13.9 0.7 compare_select_fusion.3
  14.6 0.9 copy.147
  16.1 0.9 copy.146
  17.6 0.9 copy.145
  18.5 0.6 broadcast_clamp_fusion.2
  19.1 0.6 broadcast_clamp_fusion.3
  19.8 0.7 compare_select_fusion.2
  20.6 2.6 copy.112
  23.2 2.7 copy.111
  26.0 109.9 %all-reduce.4.cloned.1.call-done = f32[16,8192]{0,1:T(8,128)} async-done(((f32[16,8192]{0,1:T(8,128)}), f32[16,8192]{0,1:T(8,128)}) %all-reduce.4.cloned.1.call-update) | async-done | bytes 524304 | tf_op jit(solution)/shard_map/psum | solution.py:58
  135.9 5.9 add.165
  141.8 21.4 %scatter_custom_fusion = f32[16,8192]{0,1:T(8,128)} fusion(f32[16,8192]{0,1:T(8,128)} %copy.112, s32[2048]{0:T(1024)S(1)} %get-tuple-element.58, f32[16,8192]{0,1:T(8,128)} %add.165, s32[2048]{0:T(1024)} %get-tuple-element.55), kind=kCustom, calls=%fused_computation.42 | custom fusion | bytes 524288 | tf_op jit(solution)/shard_map/scatter | solution.py:62
  163.2 7.6 gather_fusion
  170.8 1.3 select_bitcast_fusion
  172.2 0.8 slice_bitcast_fusion
  173.0 0.9 copy.154
  173.9 110.3 %all-reduce.6.cloned.1.call-done = f32[16,2048]{0,1:T(8,128)} async-done(((f32[16,2048]{0,1:T(8,128)}), f32[16,2048]{0,1:T(8,128)}) %all-reduce.6.cloned.1.call-update) | async-done | bytes 131088 | tf_op jit(solution)/shard_map/psum | solution.py:67
  284.1 10.2 scatter_custom_fusion.1
  294.4 56.9 %gather_fusion.4 = f32[16384,16]{1,0:T(8,128)} fusion(f32[16,8192]{0,1:T(8,128)} %scatter_custom_fusion.1, s32[16384]{0:T(1024)S(1)} %copy-done.9), kind=kCustom, calls=%fused_computation.5 | custom fusion | bytes 2162688 | tf_op jit(solution)/shard_map/gather | solution.py:72
  351.3 5.1 copy.120
  356.5 57.0 %gather_fusion.3 = f32[16384,16]{1,0:T(8,128)} fusion(f32[16,8192]{0,1:T(8,128)} %scatter_custom_fusion.1, s32[16384]{0:T(1024)S(1)} %copy-done.10), kind=kCustom, calls=%fused_computation.4 | custom fusion | bytes 2162688 | tf_op jit(solution)/shard_map/gather | solution.py:72
  413.4 6.0 copy.118
  419.4 56.9 %gather_fusion.2 = f32[16384,16]{1,0:T(8,128)} fusion(f32[16,8192]{0,1:T(8,128)} %scatter_custom_fusion.1, s32[16384]{0:T(1024)S(1)} %copy-done.11), kind=kCustom, calls=%fused_computation.3 | custom fusion | bytes 2162688 | tf_op jit(solution)/shard_map/gather | solution.py:72
  476.4 6.0 copy.116
  482.4 56.9 %gather_fusion.1 = f32[16384,16]{1,0:T(8,128)} fusion(f32[16,8192]{0,1:T(8,128)} %scatter_custom_fusion.1, s32[16384]{0:T(1024)S(1)} %copy-done.12), kind=kCustom, calls=%fused_computation.2 | custom fusion | bytes 2162688 | tf_op jit(solution)/shard_map/gather | solution.py:70
  539.4 6.0 copy.114
  545.4 3.1 fusion.16
  548.6 5.4 copy.121
  553.9 6.4 reshape.385
  560.4 6.5 all-to-all-start
  567.1 10.3 all-to-all-done
  577.4 4.1 reshape.386
  581.5 4.4 copy.123
  586.5 0.9 copy.148
  587.4 2.6 convolution_add_fusion.1
  590.1 3.2 convolution_add_fusion.2
  593.3 0.8 divide_subtract_fusion
  594.1 2.6 fusion.20
  596.7 4.7 fusion.3
  601.4 1.1 copy.149
  602.6 1.3 copy.125
  603.9 3.6 all-to-all-start.1
  607.7 0.9 copy.151
  608.6 8.6 all-to-all-done.1
  617.9 1.8 fusion.11
  619.6 5.9 copy.127
  625.5 4.6 copy.128
  630.1 4.6 copy.129
  634.7 4.6 copy.130
  639.3 89.7 %scatter_custom_fusion.2 = f32[16,8192]{0,1:T(8,128)} fusion(s32[16384]{0:T(1024)} %bitcast.166, f32[16384,16]{1,0:T(8,128)} %copy.127, f32[]{:T(128)} %constant.13.clone.1), kind=kCustom, calls=%fused_computation.20 | custom fusion | flops 262144 | bytes 524800 | tf_op jit(solution)/shard_map/scatter-add | solution.py:87
  729.1 82.9 %scatter_fusion = f32[16,8192]{0,1:T(8,128)} fusion(f32[16,8192]{0,1:T(8,128)} %scatter_custom_fusion.2, s32[16384]{0:T(1024)S(1)} %bitcast.151, f32[16384,16]{1,0:T(8,128)} %copy.128), kind=kCustom, calls=%fused_computation.9 | custom fusion | flops 262144 | bytes 3211264 | tf_op jit(solution)/shard_map/scatter-add | solution.py:87
  811.9 82.9 %scatter_fusion.1 = f32[16,8192]{0,1:T(8,128)} fusion(f32[16,8192]{0,1:T(8,128)} %scatter_fusion, s32[16384]{0:T(1024)S(1)} %bitcast.152, f32[16384,16]{1,0:T(8,128)} %copy.129), kind=kCustom, calls=%fused_computation.10 | custom fusion | flops 262144 | bytes 3211264 | tf_op jit(solution)/shard_map/scatter-add | solution.py:87
  894.8 82.9 %scatter_fusion.2 = f32[16,8192]{0,1:T(8,128)} fusion(f32[16,8192]{0,1:T(8,128)} %scatter_fusion.1, s32[16384]{0:T(1024)S(1)} %bitcast.153, f32[16384,16]{1,0:T(8,128)} %copy.130), kind=kCustom, calls=%fused_computation.11 | custom fusion | flops 262144 | bytes 3211264 | tf_op jit(solution)/shard_map/scatter-add | solution.py:87
  977.6 3.7 convert_element_type.78
  981.4 3.5 copy.131
  984.9 110.2 %all-reduce.8.cloned.1.call-done = bf16[16,8192]{0,1:T(8,128)(2,1)} async-done(((bf16[16,8192]{0,1:T(8,128)(2,1)}), bf16[16,8192]{0,1:T(8,128)(2,1)}) %all-reduce.8.cloned.1.call-update) | async-done | bytes 262160 | tf_op jit(solution)/shard_map/psum | solution.py:90
  1095.0 2.7 fusion.2
  1097.8 60.3 %psum.31 = f32[8192]{0:T(1024)S(1)} all-reduce(f32[8192]{0:T(1024)S(1)} %fusion.2), channel_id=1, replica_groups=mesh['col'=16,'grp'=16] {'col'}, use_global_device_ids=true, to_apply=%region_10.11 | all-reduce | flops 8192 | bytes 65536 | tf_op jit(solution)/shard_map/psum | solution.py:91
  1158.7 4.9 fusion.1
  1163.6 3.5 copy.132
  (78 shorter events, 4.4 us)
Async XLA Ops:
  7.2 580.3 %copy-start = (bf16[2048,512]{1,0:T(8,128)(2,1)S(1)}, bf16[2048,512]{1,0:T(8,128)(2,1)}, u32[]{:S(2)}) copy-start(bf16[2048,512]{1,0:T(8,128)(2,1)} %param.26) | copy-start | bytes 6291460
  7.2 3.9 copy-start.3
  7.2 5.2 copy-start.21
  7.2 128.7 %all-reduce.4.cloned.1.call-start = ((), (), s32[]{:S(2)}) async-start(), calls=%async_computation.2 | async-start | bytes 8388608 | tf_op jit(solution)/shard_map/psum | solution.py:58
  10.9 9.6 copy-start.18
  10.9 9.6 copy-start.4
  11.0 12.2 %copy-start.5 = (f32[16,8192]{1,0:T(8,128)S(1)}, f32[16,8192]{1,0:T(8,128)}, u32[]{:S(2)}) copy-start(f32[16,8192]{1,0:T(8,128)} %param.17) | copy-start | bytes 1572868
  11.0 273.2 %all-reduce.6.cloned.1.call-start = ((), (), s32[]{:S(2)}) async-start(), calls=%async_computation.3 | async-start | bytes 2097152 | tf_op jit(solution)/shard_map/psum | solution.py:67
  20.5 5.4 copy-start.16
  20.6 5.4 copy-start.23
  172.2 122.2 %copy-start.9 = (s32[16384]{0:T(1024)S(1)}, s32[16384]{0:T(1024)}, u32[]{:S(2)}) copy-start(s32[16384]{0:T(1024)} %broadcast_clamp_fusion) | copy-start | bytes 196612
  351.3 5.1 copy-start.10
  413.4 6.0 copy-start.11
  476.4 6.1 copy-start.12
  539.4 6.0 copy-start.6
  539.4 6.0 copy-start.7
  548.5 18.4 %copy-start.22 = (bf16[1024]{0:T(1024)(128)(2,1)S(1)}, bf16[1024]{0:T(1024)(128)(2,1)}, u32[]{:S(2)}) copy-start(bf16[1024]{0:T(1024)(128)(2,1)} %param.31) | copy-start | bytes 6148
  548.6 18.5 %copy-start.17 = (s32[1,1,8,2048]{3,2,1,0:T(8,128)S(1)}, s32[1,1,8,2048]{3,2,1,0:T(8,128)}, u32[]{:S(2)}) copy-start(s32[1,1,8,2048]{3,2,1,0:T(8,128)} %get-tuple-element.46) | copy-start | bytes 196612
  560.4 17.0 %all-to-all-start = ((bf16[16,2,8192]{2,1,0:T(2,128)(2,1)}), bf16[16,2,8192]{2,1,0:T(2,128)(2,1)S(1)}, u32[]{:S(2)}, u32[]{:S(2)}) async-start(bf16[16,2,8192]{2,1,0:T(2,128)(2,1)} %reshape.385), calls=%async_computation | async-start | bytes 1048576 | tf_op jit(solution)/shard_map/all_to_all | solution.py:74
  581.5 5.9 copy-start.20
  585.9 4.1 copy-start.24
  590.1 3.3 copy-start.25
  590.1 4.0 copy-start.2
  596.7 10.9 copy-start.15
  596.7 10.9 copy-start.14
  596.7 11.0 copy-start.13
  603.9 13.2 %all-to-all-start.1 = ((bf16[256,8,128]{2,1,0:T(8,128)(2,1)}), bf16[256,8,128]{2,1,0:T(8,128)(2,1)S(1)}, u32[]{:S(2)}, u32[]{:S(2)}) async-start(bf16[256,8,128]{2,1,0:T(8,128)(2,1)} %bitcast.24), calls=%async_computation.1 | async-start | bytes 1048576 | tf_op jit(solution)/shard_map/all_to_all | solution.py:81
  607.5 487.5 %all-reduce.8.cloned.1.call-start = ((), (), s32[]{:S(2)}) async-start(), calls=%async_computation.4 | async-start | bytes 4194304 | tf_op jit(solution)/shard_map/psum | solution.py:90
  639.3 89.8 %copy-start.8 = (s32[16384,1]{0,1:T(1,128)S(1)}, s32[16384,1]{0,1:T(1,128)}, u32[]{:S(2)}) copy-start(s32[16384,1]{0,1:T(1,128)} %compare_select_fusion.2) | copy-start | bytes 196612
  981.3 176.7 %copy-start.19 = (f32[8192]{0:T(1024)S(1)}, f32[8192]{0:T(1024)}, u32[]{:S(2)}) copy-start(f32[8192]{0:T(1024)} %param.18) | copy-start | bytes 98308
  1158.7 8.4 copy-start.1
Sparse Core Ops, SparseCore 0:
  11.1 124.7 all-reduce.3
  172.3 111.7 all-reduce.5
  981.5 113.4 all-reduce.7
where the time goes:
time: 1190 us; the launch traced here: 1170 us
  other arithmetic  368 us (31%)
  local copies, waits for them, and re-layouts  358 us (30%)
  waiting for transfers between devices  349 us (29%)
  blocking collectives  60.3 us (5%)
  between operations  14.1 us (1%)
  matrix products  13.9 us (1%)
    scatter-add x4, other arithmetic, per_device(): partial_value.at[:, bag_rows[slot].reshape(-1)]  338 us
    gather x6, local copies, waits for them, and re-layouts, per_device(): pooled = pooled + refreshed[:, bag_rows[slot]] * weights[slot][None]  188 us
    psum x1, waiting for transfers between devices, per_device(): arrived = lax.psum(fetched, 'grp')  110 us
    psum x1, waiting for transfers between devices, per_device(): lax.psum(partial_value.astype(jnp.bfloat16), 'grp').astype(jnp.float32)  110 us
    psum x1, waiting for transfers between devices, per_device(): synced = hot + lax.psum(pending[0], 'grp')  110 us
    gather x2, local copies, waits for them, and re-layouts, per_device(): pooled = refreshed[:, bag_rows[0]] * weights[0][None]  63 us
    psum x1, blocking collectives, per_device(): squares = lax.psum(jnp.sum(grad * grad, axis=0), 'col')  60.3 us
    unnamed x76, local copies, waits for them, and re-layouts  35.6 us
  transfers between devices with their start and end apart: 5, of which 5 were waited for; matrix products, arithmetic and copies ran while one was open for 2% of the time, Pallas kernels for 0%

commit v1 on v0

v1 whole, which is shorter than its diff:
```python
import jax
import jax.numpy as jnp
from jax import lax
from jax.experimental import pallas as pl
from jax.experimental.pallas import tpu as pltpu
from jax.sharding import PartitionSpec as P

E = 256
STEP = 0.2
EPS = 1e-06
MESH = pl.DeviceIdType.MESH
F32 = jnp.float32
BF16 = jnp.bfloat16
I16 = jnp.int16
I32 = jnp.int32
VMEM = pl.BlockSpec(memory_space=pltpu.VMEM)
ANY = pl.BlockSpec(memory_space=pl.ANY)
NT = (((1,), (1,)), ((), ()))
N_SEM = 288
N = 4


def plus(a, d, n):
    return lax.rem(a + d + n, n)


def column(core, a, b):
    return jnp.where(core == 0, b * 4 + a, a * 4 + b)


def pick_lanes(idx, tiles, read):
    idx = jnp.broadcast_to(idx, (8, 128))
    low = idx & 127
    high = idx >> 7
    top = jnp.zeros((8, 128), F32)
    bottom = jnp.zeros((8, 128), F32)
    for t in range(tiles):
        hit = high == t
        a, b = read(t)
        top = jnp.where(hit, jnp.take_along_axis(a, low, axis=1, mode="promise_in_bounds"), top)
        bottom = jnp.where(
            hit, jnp.take_along_axis(b, low, axis=1, mode="promise_in_bounds"), bottom
        )
    return jnp.concatenate([top, bottom], axis=0)


def split(tile):
    tile = tile.astype(F32)
    return tile[0:8], tile[8:16]


def upright(row):
    return jnp.broadcast_to(row, (128, 128)).T


def step_kernel(
    pending, table, hot, accum, slot, demote, promote, label, cross_bias, top_bias, out_weight,
    bag_rows, bag_mask, down_hbm, up_hbm, top_hbm,
    new_table, new_hot, new_accum, logits,
    down, up, top, rows_in, mask_in,
    mine, from_twin, reduced, from_ring, synced, fetched, fetched_in, arrived, match, best, slot_from,
    bags, all_synced, full, fresh, old_in, unit, units, unit_of, wide, bag_col, counts, pooled, for_twin, pooled_in, back, grads,
    evicted, home, fwd_in, side_in, lane_in, far_in, ring_out, ring_in, all_grads, squares, sums,
    load_sem, send_sem, recv_sem,
):
    col = lax.axis_index("col")
    grp = lax.axis_index("grp")
    z, core = lax.div(grp, 2), lax.rem(grp, 2)
    x, y = lax.rem(col, 4), lax.div(col, 4)
    a, b = jnp.where(core == 0, x, y), jnp.where(core == 0, y, x)
    twin = (col, grp + 1 - 2 * core)
    started = []
    used = [0]

    def at(da, db):
        return column(core, plus(a, da, 4), plus(b, db, 4))

    def peer(da, db):
        return (at(da, db), grp)

    def ring(d):
        return (col, plus(z, d, 8) * 2 + core)

    def group(d):
        return (col, plus(grp, d, 16))

    def plane(d):
        return (plus(col, d, 16), grp)

    def go(src, dst, to):
        k = used[0]
        used[0] += 1
        copy = pltpu.make_async_remote_copy(
            src_ref=src, dst_ref=dst, send_sem=send_sem.at[k], recv_sem=recv_sem.at[k],
            device_id=to, device_id_type=MESH,
        )
        copy.start()
        started.append(copy)
        return k

    def landed(k, dst):
        pltpu.make_async_remote_copy(
            src_ref=dst, dst_ref=dst, send_sem=send_sem.at[k], recv_sem=recv_sem.at[k],
            device_id=twin, device_id_type=MESH,
        ).wait_recv()

    loads = [
        pltpu.make_async_copy(src, dst, load_sem.at[i])
        for i, (src, dst) in enumerate(
            (
                (bag_rows.at[:, :, pl.ds(pl.multiple_of(col * 128, 128), 128)], rows_in),
                (bag_mask.at[:, :, pl.ds(pl.multiple_of(col * 128, 128), 128)], mask_in),
                (down_hbm, down),
                (up_hbm, up),
                (top_hbm, top),
            )
        )
    ]
    for load in loads:
        load.start()
    barrier = pltpu.get_barrier_semaphore()
    others = [group(d) for d in range(1, 16)] + [plane(d) for d in range(1, 16)]
    for other in others:
        pl.semaphore_signal(barrier, inc=1, device_id=other, device_id_type=MESH)

    def lanes_of(h, p):
        return pl.ds(pl.multiple_of(h * 4096 + p * 512, 512), 512)

    @pl.loop(0, 16)
    def _(i):
        h, p = lax.div(i, 8), lax.rem(i, 8)
        mine[h, p] = pending[:, lanes_of(h, p)]

    best[...] = jnp.full_like(best, -1)

    @pl.loop(0, 16)
    def _(t):
        dem, slo = upright(demote[pl.ds(t, 1), :]), upright(slot[pl.ds(t, 1), :])
        for j in range(16):
            hit = jnp.where(dem == promote[j : j + 1, :], slo, -1)
            best[j] = jnp.maximum(best[j], jnp.max(hit.reshape(16, 8, 128), axis=0))

    for j in range(16):
        match[j : j + 1, :] = jnp.max(best[j], axis=0, keepdims=True)

    @pl.loop(0, 16)
    def _(t):
        idx = promote[pl.ds(t, 1), :] - grp * 8192
        idx = jnp.where((match[pl.ds(t, 1), :] < 0) & (idx >= 0) & (idx < 8192), idx, -1)
        fetched[t] = pick_lanes(
            idx, 64, lambda s: split(table[:, s * 128 : (s + 1) * 128])
        )

    loads[0].wait()
    loads[1].wait()
    bags[0] = jnp.where(mask_in[...] > 0, rows_in[...], -1)
    pl.semaphore_wait(barrier, len(others))

    k_twin = go(mine.at[1 - core], from_twin, twin)

    k_bags = go(bags.at[0], bags.at[1], twin)

    def stand(which):
        @pl.loop(0, 32)
        def _(i):
            l, f = lax.div(i, 8), lax.rem(i, 8)
            row = upright(bags[which, l, pl.ds(f, 1), :] - core * 4096)
            bag_col[l, pl.ds(pl.multiple_of(which * 1024 + f * 128, 128), 128), :] = row.astype(I16)

    stand(0)
    landed(k_twin, from_twin)
    reduced[...] = mine[core] + from_twin[...]
    k_ring = [go(reduced.at[plus(z, d, 8)], from_ring.at[d], ring(d)) for d in range(1, 8)]

    def count(lo, hi):
        @pl.loop(lo, hi)
        def _(i):
            r = pl.ds(pl.multiple_of(i * 16, 16), 16)
            lane = lax.broadcasted_iota(I32, (16, 128), 1)
            idx = [bag_col[l, r, :].astype(I32) for l in range(4)]
            low = [jnp.where((v & 127) == lane, 1.0, 0.0).astype(BF16) for v in idx]
            high = [(v >> 7).astype(F32).astype(BF16) for v in idx]
            zero = jnp.zeros((16, 128), BF16)
            for t in range(32):
                acc = None
                for l in range(4):
                    hit = jnp.where(high[l] == BF16(t), low[l], zero)
                    acc = hit if acc is None else acc + hit
                counts[r, t * 128 : (t + 1) * 128] = acc

    def origin(ids, first, places, half_rows):
        ids = ids - first
        lane = ids & 127
        high = ids >> 7
        j = lax.broadcasted_iota(I32, (1, 2048), 1)
        sub = lax.broadcasted_iota(I32, (128, 2048), 0)
        here = sub == lane
        major = jnp.where(here, (j >> 7).astype(F32), 0.0).astype(BF16)
        minor = jnp.where(here, (j & 127).astype(F32) + 1.0, 0.0).astype(BF16)
        rows = lax.broadcasted_iota(I32, (half_rows, 2048), 0)
        pick = jnp.where(rows == high, 1.0, 0.0).astype(BF16)
        major = lax.dot_general(pick, major, NT, preferred_element_type=F32)
        minor = lax.dot_general(pick, minor, NT, preferred_element_type=F32)
        return (major * 128.0 + minor).astype(I32) - 1

    def flat(ref):
        return jnp.concatenate([ref[t : t + 1, :] for t in range(16)], axis=1)

    slot_from[...] = origin(flat(slot), core * 4096, 4096, 32)
    home[...] = origin(flat(demote), grp * 8192, 8192, 64)
    count(0, 40)
    total = reduced[z]
    for d in range(1, 8):
        landed(k_ring[d - 1], from_ring.at[d])
        total = total + from_ring[d]
    base = core * 4096 + z * 512
    synced[...] = total + hot[:, pl.ds(pl.multiple_of(base, 512), 512)]

    @pl.loop(0, 16)
    def _(t):
        again = match[pl.ds(t, 1), :] - base
        value = pick_lanes(again, 4, lambda s: split(synced[:, s * 128 : (s + 1) * 128]))
        fetched[t] = value + fetched[t]

    k_fet = [go(fetched.at[plus(grp, d, 16)], fetched_in.at[d], group(d)) for d in range(1, 16)]
    all_synced[grp] = synced[...]
    k_syn = [go(all_synced.at[grp], all_synced.at[grp], ring(d)) for d in range(1, 8)]
    k_hand = [go(all_synced.at[grp], all_synced.at[grp], twin)]
    landed(k_bags, bags.at[1])
    stand(1)
    count(40, 84)
    mine_now = fetched[grp]
    for d in range(1, 16):
        landed(k_fet[d - 1], fetched_in.at[d])
        mine_now = mine_now + fetched_in[d]
    arrived[grp] = mine_now
    k_arr = [go(arrived.at[grp], arrived.at[grp], group(d)) for d in range(1, 16)]
    count(84, 128)
    for d in range(1, 8):
        there = all_synced.at[plus(z, -d, 8) * 2 + core]
        landed(k_syn[d - 1], there)
        k_hand.append(go(there, there, twin))
    for d in range(1, 16):
        landed(k_arr[d - 1], arrived.at[plus(grp, -d, 16)])

    def renew(lo, hi):
        @pl.loop(lo, hi)
        def _(p):
            for i in range(4):
                idx = slot_from[pl.ds(p * 4 + i, 1), :]
                lanes = slice(i * 128, (i + 1) * 128)
                picked = pick_lanes(idx, 16, lambda s: split(arrived[s]))
                old = all_synced[p * 2 + core, :, lanes]
                value = jnp.where(jnp.broadcast_to(idx, (16, 128)) >= 0, picked, old)
                fresh[p, :, lanes] = value
                unit[pl.ds(p * 4 + i, 1), :] = jnp.max(jnp.abs(value), axis=0, keepdims=True)

    def encode():
        units[col] = (jnp.maximum(unit[...], 1e-30) * (1.008 / 32000.0)).astype(BF16)
        unit[...] = 1.0 / units[col].astype(F32)

        @pl.loop(0, 8)
        def _(p):
            for i in range(4):
                lanes = slice(i * 128, (i + 1) * 128)
                code = jnp.round(fresh[p, :, lanes] * unit[pl.ds(p * 4 + i, 1), :])
                full[col, p, :, lanes] = code.astype(I32).astype(I16)

    def decode(c):
        unit_of[...] = units[c].astype(F32)

        @pl.loop(0, 8)
        def _(p):
            for i in range(4):
                lanes = slice(i * 128, (i + 1) * 128)
                value = full[c, p, :, lanes].astype(I32).astype(F32)
                value = value * unit_of[pl.ds(p * 4 + i, 1), :]
                high = value.astype(BF16)
                wide[0, p, c, :, lanes] = high
                wide[1, p, c, :, lanes] = (value - high.astype(F32)).astype(BF16)

    def demoted(lo, hi):
        @pl.loop(lo, hi)
        def _(t):
            evicted[t] = pick_lanes(
                slot[pl.ds(t, 1), :], 64,
                lambda s: split(
                    all_synced[
                        (s % 32 // 4) * 2 + s // 32, :, (s % 4) * 128 : (s % 4 + 1) * 128
                    ]
                ),
            )

    def table_out(lo, hi):
        @pl.loop(lo, hi)
        def _(q):
            for u in range(4):
                lanes = pl.ds(pl.multiple_of(q * 512 + u * 128, 128), 128)
                idx = home[pl.ds(q * 4 + u, 1), :]
                picked = pick_lanes(idx, 16, lambda s: (evicted[s, 0:8, :], evicted[s, 8:16, :]))
                new_table[:, lanes] = jnp.where(
                    jnp.broadcast_to(idx, (16, 128)) >= 0, picked, table[:, lanes]
                )

    def widen():
        half = pl.ds(0, 4), pl.ds(4, 4)

        def block(da, db, which=None):
            ref = full.at[at(da, db)]
            return ref if which is None else ref.at[half[which]]

        def pass_on(ref, to):
            return go(ref, ref, to)

        def along_b(da):
            return pass_on(block(da, 0), peer(0, 1)), pass_on(block(da, 0), peer(0, -1))

        right = pass_on(block(0, 0), peer(1, 0))
        left = pass_on(block(0, 0), peer(-1, 0))
        pairs = {0: along_b(0)}
        more = {}

        def along_b_more(da):
            landed(pairs[da][0], block(da, -1))
            first = pass_on(block(da, -1, 0), peer(0, 1))
            landed(pairs[da][1], block(da, 1))
            more[da] = first, pass_on(block(da, 1, 1), peer(0, -1))
            decode(at(da, -1))
            decode(at(da, 1))

        yield
        decode(col)
        landed(right, block(-1, 0))
        on_right = pass_on(block(-1, 0, 0), peer(1, 0))
        pairs[-1] = along_b(-1)
        yield
        landed(left, block(1, 0))
        on_left = pass_on(block(1, 0, 1), peer(-1, 0))
        pairs[1] = along_b(1)
        yield
        along_b_more(0)
        yield
        landed(on_right, block(2, 0, 0))
        landed(on_left, block(2, 0, 1))
        pairs[2] = along_b(2)
        for da in (-1, 1, 2):
            decode(at(da, 0))
        for da in (-1, 1, 2):
            yield
            along_b_more(da)
        for da in (0, -1, 1, 2):
            yield
            landed(more[da][0], block(da, 2, 0))
            landed(more[da][1], block(da, 2, 1))
            decode(at(da, 2))

    def look(first, out):
        acc = None
        for p in range(8):
            some = counts[pl.ds(pl.multiple_of(first, 256), 256), p * 512 : (p + 1) * 512]
            for k in range(2):
                term = lax.dot_general(
                    some, wide[k, p].reshape(256, 512), NT, preferred_element_type=F32
                )
                acc = term if acc is None else acc + term
        out[...] = acc

    renew(0, 8)
    encode()
    travel = widen()
    next(travel)
    k_unit = [go(units.at[col], units.at[col], plane(d)) for d in range(1, 16)]
    k_old = go(fresh, old_in, twin)
    for d in range(8):
        landed(k_hand[d], all_synced.at[plus(z, -d, 8) * 2 + 1 - core])
    next(travel)
    next(travel)
    for d in range(1, 16):
        landed(k_unit[d - 1], units.at[plus(col, -d, 16)])
    for _ in travel:
        pass

    k_pool = []
    for m in range(4):
        look(1024 + m * 256, for_twin.at[m])
        k_pool.append(go(for_twin.at[m], pooled_in.at[m], twin))

    @pl.loop(0, 4)
    def _(m):
        look(m * 256, pooled.at[m])

    for m in range(4):
        landed(k_pool[m], pooled_in.at[m])

    for load in loads[2:]:
        load.wait()
    both = [(pooled[m] + pooled_in[m]).astype(BF16) for m in range(4)]
    x0 = jnp.concatenate(
        [both[f // 2][f % 2 * 128 : f % 2 * 128 + 128] for f in range(8)], axis=1
    )
    low = jnp.dot(x0, down[...], preferred_element_type=F32).astype(BF16)
    gate = jnp.dot(low, up[...], preferred_element_type=F32) + cross_bias[...]
    wide0 = x0.astype(F32)
    x1 = (wide0 * gate + wide0).astype(BF16)
    pre = jnp.dot(x1, top[...], preferred_element_type=F32) + top_bias[...]
    sig = jax.nn.sigmoid(pre)
    hidden = (pre * sig).astype(BF16).astype(F32)
    weight = out_weight[...].astype(F32).reshape(1, 1024)
    logit = jnp.sum(hidden * weight, axis=1, keepdims=True)
    across = jnp.broadcast_to(logit, (128, 128)).T
    logits[...] = across[0:1, :]
    dlogit = jax.nn.sigmoid(across) - label[...].astype(F32)
    dlogit = dlogit.T[:, 0:1]
    slope = sig * (1.0 + pre * (1.0 - sig))
    dhidden = (dlogit * weight * slope).astype(BF16)
    dx1 = lax.dot_general(dhidden, top[...], NT, preferred_element_type=F32)
    dgate = (dx1 * wide0).astype(BF16)
    dlow = lax.dot_general(dgate, up[...], NT, preferred_element_type=F32).astype(BF16)
    k_back = []
    for c in range(4):
        lanes = slice(c * 512, (c + 1) * 512)
        dx0 = dx1[:, lanes] * (gate[:, lanes] + 1.0) + lax.dot_general(
            dlow, down[lanes, :], NT, preferred_element_type=F32
        )
        for f in range(2):
            back[c, :, f * 128 : (f + 1) * 128] = dx0[:, f * 256 : (f + 1) * 256].T.astype(BF16)
        k_back.append(go(back.at[c], back.at[4 + c], twin))

    for c in range(4):
        landed(k_back[c], back.at[4 + c])

    def slopes(lo, hi):
        @pl.loop(lo, hi)
        def _(p):
            lanes = pl.ds(pl.multiple_of(p * 512, 512), 512)
            acc = None
            for c in range(8):
                term = jnp.dot(
                    back[c], counts[c * 256 : (c + 1) * 256, lanes], preferred_element_type=F32
                )
                acc = term if acc is None else acc + term
            grads[:, p] = acc.astype(BF16).reshape(16, 16, 512)

    def add(ref, other):
        ref[...] = (ref[...].astype(F32) + other[...].astype(F32)).astype(BF16)

    order = [(da, db) for da in (2, 1, -1, 0) for db in (2, 1, -1, 0)]

    def narrow(s):
        whole = pl.ds(s * N, N)
        lo, hi = pl.ds(s * N, N // 2), pl.ds(s * N + N // 2, N // 2)
        few = pl.ds(s * N // 2, N // 2)
        ways = [{} for _ in range(4)]
        last = {}

        def first_part(i):
            for j in range(4):
                k = i * 4 + j
                where = at(*order[k])
                if j == 0:
                    ways[i][0] = go(grads.at[where, lo], fwd_in.at[i, 0, few], peer(0, 1))
                    ways[i][1] = go(grads.at[where, hi], fwd_in.at[i, 1, few], peer(0, -1))
                if j == 1:
                    ways[i][2] = go(grads.at[where, hi], side_in.at[i, 0, hi], peer(0, 1))
                if j == 2:
                    ways[i][3] = go(grads.at[where, lo], side_in.at[i, 1, lo], peer(0, -1))

        def second_part(i):
            landed(ways[i][0], fwd_in.at[i, 0, few])
            add(grads.at[at(*order[i * 4 + 1]), lo], fwd_in.at[i, 0, few])
            ways[i][4] = go(grads.at[at(*order[i * 4 + 1]), lo], side_in.at[i, 0, lo], peer(0, 1))
            landed(ways[i][1], fwd_in.at[i, 1, few])
            add(grads.at[at(*order[i * 4 + 2]), hi], fwd_in.at[i, 1, few])
            ways[i][5] = go(grads.at[at(*order[i * 4 + 2]), hi], side_in.at[i, 1, hi], peer(0, -1))

        def third_part(i):
            landed(ways[i][2], side_in.at[i, 0, hi])
            landed(ways[i][3], side_in.at[i, 1, lo])
            landed(ways[i][4], side_in.at[i, 0, lo])
            landed(ways[i][5], side_in.at[i, 1, hi])
            where = at(*order[i * 4 + 3])
            grads[where, whole] = (
                grads[where, whole].astype(F32)
                + side_in[i, 0, whole].astype(F32)
                + side_in[i, 1, whole].astype(F32)
            ).astype(BF16)

        def last_axis(i):
            where = at(*order[i * 4 + 3])
            if i == 0:
                last[0] = go(grads.at[where, lo], far_in.at[0, few], peer(1, 0))
                last[1] = go(grads.at[where, hi], far_in.at[1, few], peer(-1, 0))
            if i == 1:
                last[2] = go(grads.at[where, hi], lane_in.at[0, hi], peer(1, 0))
                landed(last[0], far_in.at[0, few])
                add(grads.at[where, lo], far_in.at[0, few])
                last[4] = go(grads.at[where, lo], lane_in.at[0, lo], peer(1, 0))
            if i == 2:
                last[3] = go(grads.at[where, lo], lane_in.at[1, lo], peer(-1, 0))
                landed(last[1], far_in.at[1, few])
                add(grads.at[where, hi], far_in.at[1, few])
                last[5] = go(grads.at[where, hi], lane_in.at[1, hi], peer(-1, 0))

        def begin():
            for i in range(4):
                first_part(i)

        def more(*parts):
            for i in parts:
                second_part(i)

        def turn(i):
            third_part(i)
            last_axis(i)

        def finish():
            turn(3)
            landed(last[2], lane_in.at[0, hi])
            landed(last[3], lane_in.at[1, lo])
            landed(last[4], lane_in.at[0, lo])
            landed(last[5], lane_in.at[1, hi])
            ring_out[whole] = (
                grads[col, whole].astype(F32)
                + lane_in[0, whole].astype(F32)
                + lane_in[1, whole].astype(F32)
            ).astype(BF16)

        return begin, more, turn, finish

    slopes(0, 4)
    begin0, more0, turn0, finish0 = narrow(0)
    begin1, more1, turn1, finish1 = narrow(1)
    begin0()
    slopes(4, 6)
    more0(0, 1)
    slopes(6, 8)
    begin1()
    more0(2, 3)
    turn0(0)
    turn0(1)
    more1(0, 1)
    turn0(2)
    more1(2, 3)
    turn1(0)
    turn1(1)
    finish0()
    turn1(2)
    finish1()

    k_ring = [go(ring_out.at[plus(z, d, 8)], ring_in.at[d], ring(d)) for d in range(1, 8)]
    demoted(0, 16)
    grad = ring_out[z].astype(F32)
    for d in range(1, 8):
        landed(k_ring[d - 1], ring_in.at[d])
        grad = grad + ring_in[d].astype(F32)
    square = jnp.sum(grad * grad, axis=0, keepdims=True)
    square = [square[:, i * 128 : (i + 1) * 128] for i in range(4)]
    squares[col] = jnp.concatenate(square + square, axis=0)
    k_sq = [go(squares.at[col], squares.at[col], plane(d)) for d in range(1, 16)]
    all_grads[grp] = grad.astype(BF16)
    k_all = [go(all_grads.at[grp], all_grads.at[grp], ring(d)) for d in range(1, 8)]
    k_hand = [go(all_grads.at[grp], all_grads.at[grp], twin)]
    table_out(0, 9)
    for d in range(1, 16):
        landed(k_sq[d - 1], squares.at[plus(col, -d, 16)])
    before = accum[pl.ds(core * 32 + z * 4, 4), :]
    sums[grp] = jnp.concatenate([before, before], axis=0) + jnp.sum(squares[...], axis=0) / E
    k_sum = [go(sums.at[grp], sums.at[grp], group(d)) for d in range(1, 16)]
    table_out(9, 16)
    for d in range(1, 8):
        there = all_grads.at[plus(z, -d, 8) * 2 + core]
        landed(k_all[d - 1], there)
        k_hand.append(go(there, there, twin))
    for d in range(8):
        landed(k_hand[d], all_grads.at[plus(z, -d, 8) * 2 + 1 - core])
    for d in range(1, 16):
        landed(k_sum[d - 1], sums.at[plus(grp, -d, 16)])
    landed(k_old, old_in)
    for h in range(2):
        for p in range(8):
            new_accum[h * 32 + p * 4 : h * 32 + p * 4 + 4, :] = sums[p * 2 + h, 0:4, :]

        @pl.loop(0, 8)
        def _(p):
            g = p * 2 + h
            for i in range(4):
                lanes = pl.ds(pl.multiple_of(h * 4096 + p * 512 + i * 128, 128), 128)
                inner = slice(i * 128, (i + 1) * 128)
                scale = STEP / jnp.sqrt(sums[g, i : i + 1, :] + EPS)
                old = jnp.where(core == h, fresh[p, :, inner], old_in[p, :, inner])
                new_hot[:, lanes] = old - all_grads[g, :, inner].astype(F32) * scale

    for copy in started:
        copy.wait_send()


def step(*args):
    dma = pltpu.SemaphoreType.DMA
    v = pltpu.VMEM
    return pl.pallas_call(
        step_kernel,
        out_shape=[
            jax.ShapeDtypeStruct((16, 8192), F32),
            jax.ShapeDtypeStruct((16, 8192), F32),
            jax.ShapeDtypeStruct((64, 128), F32),
            jax.ShapeDtypeStruct((1, 128), F32),
        ],
        in_specs=[VMEM] * 11 + [ANY] * 5,
        out_specs=[VMEM] * 4,
        scratch_shapes=[
            v((2048, 512), BF16),
            v((512, 2048), BF16),
            v((2048, 1024), BF16),
            v((4, 8, 128), I32),
            v((4, 8, 128), I32),
            v((2, 8, 16, 512), F32),
            v((8, 16, 512), F32),
            v((8, 16, 512), F32),
            v((8, 16, 512), F32),
            v((16, 512), F32),
            v((16, 16, 128), F32),
            v((16, 16, 128), F32),
            v((16, 16, 128), F32),
            v((16, 128), I32),
            v((16, 8, 128), I32),
            v((32, 128), I32),
            v((2, 4, 8, 128), I32),
            v((16, 16, 512), F32),
            v((16, 8, 16, 512), I16),
            v((8, 16, 512), F32),
            v((8, 16, 512), F32),
            v((32, 128), F32),
            v((16, 32, 128), BF16),
            v((32, 128), F32),
            v((2, 8, 16, 16, 512), BF16),
            v((4, 2048, 128), I16),
            v((2048, 4096), BF16),
            v((4, 256, 256), F32),
            v((4, 256, 256), F32),
            v((4, 256, 256), F32),
            v((8, 256, 256), BF16),
            v((16, 8, 16, 512), BF16),
            v((16, 16, 128), F32),
            v((64, 128), I32),
            v((4, 2, 4, 16, 512), BF16),
            v((4, 2, 8, 16, 512), BF16),
            v((2, 8, 16, 512), BF16),
            v((2, 4, 16, 512), BF16),
            v((8, 16, 512), BF16),
            v((8, 16, 512), BF16),
            v((16, 16, 512), BF16),
            v((16, 8, 128), F32),
            v((16, 8, 128), F32),
            dma((5,)),
            dma((N_SEM,)),
            dma((N_SEM,)),
        ],
        compiler_params=pltpu.CompilerParams(
            collective_id=0, has_side_effects=True, vmem_limit_bytes=62 << 20
        ),
    )(*args)


def hand_out_kernel(*refs):
    n = len(refs) // 2
    for i in range(n):
        refs[n + i][...] = refs[i][...]


def hand_out(*arrays):
    return pl.pallas_call(
        hand_out_kernel,
        out_shape=[jax.ShapeDtypeStruct(a.shape, a.dtype) for a in arrays],
        in_specs=[VMEM] * len(arrays),
        out_specs=[VMEM] * len(arrays),
    )(*arrays)


def per_device(
    table, hot, accum, pending, slot_ids, demote_ids, promote_ids, bag_rows, bag_mask, labels,
    cross_down, cross_up, cross_bias, top_weight, top_bias, out_weight,
):
    outputs = step(
        pending[0], table, hot, accum.reshape(64, 128), slot_ids.reshape(16, 128),
        demote_ids.reshape(16, 128), promote_ids.reshape(16, 128), labels, cross_bias[None],
        top_bias[None], out_weight, bag_rows, bag_mask, cross_down, cross_up, top_weight,
    )
    new_table, new_hot, new_accum, logits = hand_out(*outputs)
    return new_table, new_hot, new_accum.reshape(8192), logits


def solution(mesh):
    return jax.shard_map(
        per_device,
        mesh=mesh,
        in_specs=(
            P("col", "grp"), P("col", None), P(), P("grp", "col", None), P(), P(), P(),
            P(None, None, "grp"), P(None, None, "grp"), P("col", "grp"),
            P(), P(), P(), P(), P(), P(),
        ),
        out_specs=(P("col", "grp"), P("col", None), P(), P("col", "grp")),
        check_vma=False,
    )
```

time: 1190 us -> 133 us (0.11); the launches traced: 1170 us -> 133 us
  other arithmetic: 368 us -> 0 us
  local copies, waits for them, and re-layouts: 358 us -> 0 us
  waiting for transfers between devices: 349 us -> 0 us
  Pallas kernels: 0 us -> 132 us
  blocking collectives: 60.3 us -> 0 us
  matrix products: 13.9 us -> 0 us
  between operations: 14.1 us -> 0.65 us
    scatter-add x4 -> x0, other arithmetic: 338 us -> none  [per_device(): partial_value.at[:, bag_rows[slot].reshape(-1)]]
    psum x3 -> x0, waiting for transfers between devices: 330 us -> none  [the longest x1 110 us: per_device(): arrived = lax.psum(fetched, 'grp')]
    gather x9 -> x0, local copies, waits for them, and re-layouts: 259 us -> none  [the longest x6 188 us: per_device(): pooled = pooled + refreshed[:, bag_rows[slot]] * weights[slot][None]]
    pallas_call x0 -> x2, Pallas kernels: none -> 132 us  [the longest x1 130 us: step(): pl.pallas_call(step_kernel, out_shape=[jax.ShapeDtypeStruct((16, 8192), F...]
    psum x1 -> x0, blocking collectives: 60.3 us -> none  [per_device(): squares = lax.psum(jnp.sum(grad * grad, axis=0), 'col')]
    unnamed x76 -> x0, local copies, waits for them, and re-layouts: 35.6 us -> none
    scatter x2 -> x0, local copies, waits for them, and re-layouts: 31.6 us -> none  [the longest x1 21.4 us: per_device(): new_table = table.at[:, demote_target].set(synced[:, slot_ids], mode='drop')]
    mul x4 -> x0, local copies, waits for them, and re-layouts: 19.7 us -> none  [per_device(): terms = returned * weights[slot][None]]
  transfers between devices with their start and end apart: 5 -> 0, of which waited for: 5 -> 0; matrix products, arithmetic and copies ran while one was open for 2% -> 0% of each run, Pallas kernels for 0% -> 0%
where the time goes in v1:
time: 133 us
  Pallas kernels  132 us (99%)
    pallas_call x1, Pallas kernels, step(): pl.pallas_call(step_kernel, out_shape=[jax.ShapeDtypeStruct((16, 8192), F...  130 us

profile of v1, /device:TPU:1, one launch (start us, length us, event | category | flops | bytes accessed | tf_op | source)
XLA Modules:
  0.0 133.1 jit_solution(179762415224708018)
XLA Ops:
  0.6 130.2 %shard_map.183 = (f32[16,8192]{1,0:T(8,128)}, f32[16,8192]{1,0:T(8,128)}, f32[64,128]{1,0:T(8,128)}, f32[1,128]{1,0:T(1,128)}) custom-call(f32[16,8192]{1,0:T(8,128)} %bitcast.8, f32[16,8192]{1,0:T(8,128)} %table.1, f32[16,8192]{1,0:T(8,128)} %hot.1, f32[64,128]{1,0:T(8,128)} %bitcast.9, s32[16,128]{1,0:T(8,128)} %bitcast.10, s32[16,128]{1,0:T(8,128)} %bitcast.11, ...), custom_call_target="tpu_custom_call" | custom-call | tf_op jit(solution)/shard_map/pallas_call | solution.py:600
  130.9 2.2 %shard_map.184 = (f32[16,8192]{1,0:T(8,128)}, f32[16,8192]{1,0:T(8,128)}, f32[64,128]{1,0:T(8,128)}, f32[1,128]{1,0:T(1,128)}) custom-call(f32[16,8192]{1,0:T(8,128)} %get-tuple-element.12.refs_0_, f32[16,8192]{1,0:T(8,128)} %get-tuple-element.13.refs_1_, f32[64,128]{1,0:T(8,128)} %get-tuple-element.14.refs_2_, f32[1,128]{1,0:T(1,128)} %get-tuple-element.15.refs_3_), custom_call_target="tpu_custom_call" | custom-call | tf_op jit(solution)/shard_map/pallas_call | solution.py:671

commit v2 on v1

--- a/solution.py
+++ b/solution.py
@@ -255,21 +255,18 @@
                 fresh[p, :, lanes] = value
                 unit[pl.ds(p * 4 + i, 1), :] = jnp.max(jnp.abs(value), axis=0, keepdims=True)
 
-    def encode():
-        units[col] = (jnp.maximum(unit[...], 1e-30) * (1.008 / 32000.0)).astype(BF16)
-        unit[...] = 1.0 / units[col].astype(F32)
-
-        @pl.loop(0, 8)
+    def encode(s):
+        @pl.loop(s * N, s * N + N)
         def _(p):
             for i in range(4):
                 lanes = slice(i * 128, (i + 1) * 128)
                 code = jnp.round(fresh[p, :, lanes] * unit[pl.ds(p * 4 + i, 1), :])
                 full[col, p, :, lanes] = code.astype(I32).astype(I16)
 
-    def decode(c):
+    def decode(c, s):
         unit_of[...] = units[c].astype(F32)
 
-        @pl.loop(0, 8)
+        @pl.loop(s * N, s * N + N)
         def _(p):
             for i in range(4):
                 lanes = slice(i * 128, (i + 1) * 128)
@@ -302,12 +299,12 @@
                     jnp.broadcast_to(idx, (16, 128)) >= 0, picked, table[:, lanes]
                 )
 
-    def widen():
-        half = pl.ds(0, 4), pl.ds(4, 4)
+    def widen(s):
+        whole = pl.ds(s * N, N)
+        half = pl.ds(s * N, N // 2), pl.ds(s * N + N // 2, N // 2)
 
         def block(da, db, which=None):
-            ref = full.at[at(da, db)]
-            return ref if which is None else ref.at[half[which]]
+            return full.at[at(da, db), whole if which is None else half[which]]
 
         def pass_on(ref, to):
             return go(ref, ref, to)
@@ -325,11 +322,11 @@
             first = pass_on(block(da, -1, 0), peer(0, 1))
             landed(pairs[da][1], block(da, 1))
             more[da] = first, pass_on(block(da, 1, 1), peer(0, -1))
-            decode(at(da, -1))
-            decode(at(da, 1))
+            decode(at(da, -1), s)
+            decode(at(da, 1), s)
 
         yield
-        decode(col)
+        decode(col, s)
         landed(right, block(-1, 0))
         on_right = pass_on(block(-1, 0, 0), peer(1, 0))
         pairs[-1] = along_b(-1)
@@ -344,7 +341,7 @@
         landed(on_left, block(2, 0, 1))
         pairs[2] = along_b(2)
         for da in (-1, 1, 2):
-            decode(at(da, 0))
+            decode(at(da, 0), s)
         for da in (-1, 1, 2):
             yield
             along_b_more(da)
@@ -352,42 +349,63 @@
             yield
             landed(more[da][0], block(da, 2, 0))
             landed(more[da][1], block(da, 2, 1))
-            decode(at(da, 2))
-
-    def look(first, out):
+            decode(at(da, 2), s)
+
+    def look(s, first, out):
         acc = None
-        for p in range(8):
+        for p in range(s * N, s * N + N):
             some = counts[pl.ds(pl.multiple_of(first, 256), 256), p * 512 : (p + 1) * 512]
             for k in range(2):
                 term = lax.dot_general(
                     some, wide[k, p].reshape(256, 512), NT, preferred_element_type=F32
                 )
                 acc = term if acc is None else acc + term
-        out[...] = acc
+        if s == 0:
+            out[...] = acc
+        else:
+            out[...] += acc
 
     renew(0, 8)
-    encode()
-    travel = widen()
-    next(travel)
+    units[col] = (jnp.maximum(unit[...], 1e-30) * (1.008 / 32000.0)).astype(BF16)
+    unit[...] = 1.0 / units[col].astype(F32)
+    encode(0)
+    one, two = widen(0), widen(1)
+    next(one)
     k_unit = [go(units.at[col], units.at[col], plane(d)) for d in range(1, 16)]
+    encode(1)
+    next(two)
     k_old = go(fresh, old_in, twin)
     for d in range(8):
         landed(k_hand[d], all_synced.at[plus(z, -d, 8) * 2 + 1 - core])
-    next(travel)
-    next(travel)
+    next(one)
+    next(one)
+    next(two)
+    next(two)
     for d in range(1, 16):
         landed(k_unit[d - 1], units.at[plus(col, -d, 16)])
-    for _ in travel:
+    next(one)
+    next(one)
+    next(two)
+    next(one)
+    next(one)
+    next(two)
+    for _ in one:
+        pass
+    chunks = [(for_twin, 1024, m) for m in range(4)] + [(pooled, 0, m) for m in range(4)]
+    for out, first, m in chunks:
+        look(0, first + m * 256, out.at[m])
+        next(two, None)
+    for _ in two:
         pass
 
     k_pool = []
     for m in range(4):
-        look(1024 + m * 256, for_twin.at[m])
+        look(1, 1024 + m * 256, for_twin.at[m])
         k_pool.append(go(for_twin.at[m], pooled_in.at[m], twin))
 
     @pl.loop(0, 4)
     def _(m):
-        look(m * 256, pooled.at[m])
+        look(1, m * 256, pooled.at[m])
 
     for m in range(4):
         landed(k_pool[m], pooled_in.at[m])

time: 133 us -> 133 us (level)
  no operation moved by 1% of the time
where the time goes in v2:
time: 133 us
  Pallas kernels  132 us (99%)
    pallas_call x1, Pallas kernels, step(): pl.pallas_call(step_kernel, out_shape=[jax.ShapeDtypeStruct((16, 8192), F...  130 us

profile of v2, /device:TPU:1, one launch (start us, length us, event | category | flops | bytes accessed | tf_op | source)
XLA Modules:
  0.0 132.7 jit_solution(5665333932992180865)
XLA Ops:
  0.6 129.9 %shard_map.183 = (f32[16,8192]{1,0:T(8,128)}, f32[16,8192]{1,0:T(8,128)}, f32[64,128]{1,0:T(8,128)}, f32[1,128]{1,0:T(1,128)}) custom-call(f32[16,8192]{1,0:T(8,128)} %bitcast.8, f32[16,8192]{1,0:T(8,128)} %table.1, f32[16,8192]{1,0:T(8,128)} %hot.1, f32[64,128]{1,0:T(8,128)} %bitcast.9, s32[16,128]{1,0:T(8,128)} %bitcast.10, s32[16,128]{1,0:T(8,128)} %bitcast.11, ...), custom_call_target="tpu_custom_call" | custom-call | tf_op jit(solution)/shard_map/pallas_call | solution.py:618
  130.5 2.2 %shard_map.184 = (f32[16,8192]{1,0:T(8,128)}, f32[16,8192]{1,0:T(8,128)}, f32[64,128]{1,0:T(8,128)}, f32[1,128]{1,0:T(1,128)}) custom-call(f32[16,8192]{1,0:T(8,128)} %get-tuple-element.12.refs_0_, f32[16,8192]{1,0:T(8,128)} %get-tuple-element.13.refs_1_, f32[64,128]{1,0:T(8,128)} %get-tuple-element.14.refs_2_, f32[1,128]{1,0:T(1,128)} %get-tuple-element.15.refs_3_), custom_call_target="tpu_custom_call" | custom-call | tf_op jit(solution)/shard_map/pallas_call | solution.py:689

commit v3 on v1

--- a/solution.py
+++ b/solution.py
@@ -60,7 +60,7 @@
     down, up, top, rows_in, mask_in,
     mine, from_twin, reduced, from_ring, synced, fetched, fetched_in, arrived, match, best, slot_from,
     bags, all_synced, full, fresh, old_in, unit, units, unit_of, wide, bag_col, counts, pooled, for_twin, pooled_in, back, grads,
-    evicted, home, fwd_in, side_in, lane_in, far_in, ring_out, ring_in, all_grads, squares, sums,
+    x0_ref, x1_ref, gate_ref, dx1_ref, pre_ref,    evicted, home, fwd_in, side_in, lane_in, far_in, ring_out, ring_in, all_grads, squares, sums,
     load_sem, send_sem, recv_sem,
 ):
     col = lax.axis_index("col")
@@ -381,8 +381,12 @@
         pass
 
     k_pool = []
+
+    @pl.loop(0, 4)
+    def _(m):
+        look(1024 + m * 256, for_twin.at[m])
+
     for m in range(4):
-        look(1024 + m * 256, for_twin.at[m])
         k_pool.append(go(for_twin.at[m], pooled_in.at[m], twin))
 
     @pl.loop(0, 4)
@@ -395,14 +399,30 @@
     for load in loads[2:]:
         load.wait()
     both = [(pooled[m] + pooled_in[m]).astype(BF16) for m in range(4)]
-    x0 = jnp.concatenate(
+    x0_ref[...] = jnp.concatenate(
         [both[f // 2][f % 2 * 128 : f % 2 * 128 + 128] for f in range(8)], axis=1
     )
-    low = jnp.dot(x0, down[...], preferred_element_type=F32).astype(BF16)
-    gate = jnp.dot(low, up[...], preferred_element_type=F32) + cross_bias[...]
-    wide0 = x0.astype(F32)
-    x1 = (wide0 * gate + wide0).astype(BF16)
-    pre = jnp.dot(x1, top[...], preferred_element_type=F32) + top_bias[...]
+    low = jnp.dot(x0_ref[...], down[...], preferred_element_type=F32).astype(BF16)
+
+    def lanes_at(i, size):
+        return pl.ds(pl.multiple_of(i * size, size), size)
+
+    @pl.loop(0, 4)
+    def _(i):
+        lanes = lanes_at(i, 512)
+        gate = jnp.dot(low, up[:, lanes], preferred_element_type=F32) + cross_bias[:, lanes]
+        gate_ref[:, lanes] = gate
+        wide0 = x0_ref[:, lanes].astype(F32)
+        x1_ref[:, lanes] = (wide0 * gate + wide0).astype(BF16)
+
+    @pl.loop(0, 4)
+    def _(i):
+        lanes = lanes_at(i, 256)
+        pre_ref[:, lanes] = (
+            jnp.dot(x1_ref[...], top[:, lanes], preferred_element_type=F32) + top_bias[:, lanes]
+        )
+
+    pre = pre_ref[...]
     sig = jax.nn.sigmoid(pre)
     hidden = (pre * sig).astype(BF16).astype(F32)
     weight = out_weight[...].astype(F32).reshape(1, 1024)
@@ -413,13 +433,19 @@
     dlogit = dlogit.T[:, 0:1]
     slope = sig * (1.0 + pre * (1.0 - sig))
     dhidden = (dlogit * weight * slope).astype(BF16)
-    dx1 = lax.dot_general(dhidden, top[...], NT, preferred_element_type=F32)
-    dgate = (dx1 * wide0).astype(BF16)
-    dlow = lax.dot_general(dgate, up[...], NT, preferred_element_type=F32).astype(BF16)
+
+    @pl.loop(0, 4)
+    def _(i):
+        lanes = lanes_at(i, 512)
+        dx1 = lax.dot_general(dhidden, top[lanes, :], NT, preferred_element_type=F32)
+        dx1_ref[:, lanes] = dx1
+        x1_ref[:, lanes] = (dx1 * x0_ref[:, lanes].astype(F32)).astype(BF16)
+
+    dlow = lax.dot_general(x1_ref[...], up[...], NT, preferred_element_type=F32).astype(BF16)
     k_back = []
     for c in range(4):
         lanes = slice(c * 512, (c + 1) * 512)
-        dx0 = dx1[:, lanes] * (gate[:, lanes] + 1.0) + lax.dot_general(
+        dx0 = dx1_ref[:, lanes] * (gate_ref[:, lanes] + 1.0) + lax.dot_general(
             dlow, down[lanes, :], NT, preferred_element_type=F32
         )
         for f in range(2):
@@ -640,6 +666,11 @@
             v((4, 256, 256), F32),
             v((8, 256, 256), BF16),
             v((16, 8, 16, 512), BF16),
+            v((128, 2048), BF16),
+            v((128, 2048), BF16),
+            v((128, 2048), F32),
+            v((128, 2048), F32),
+            v((128, 1024), F32),
             v((16, 16, 128), F32),
             v((64, 128), I32),
             v((4, 2, 4, 16, 512), BF16),

time: 133 us -> 131 us (0.985)
  Pallas kernels: 132 us -> 130 us
    pallas_call x1, Pallas kernels: 130 us -> 128 us  [step(): pl.pallas_call(step_kernel, out_shape=[jax.ShapeDtypeStruct((16, 8192), F...]
where the time goes in v3:
time: 131 us
  Pallas kernels  130 us (99%)
    pallas_call x1, Pallas kernels, step(): pl.pallas_call(step_kernel, out_shape=[jax.ShapeDtypeStruct((16, 8192), F...  128 us

profile of v3, /device:TPU:1, one launch (start us, length us, event | category | flops | bytes accessed | tf_op | source)
XLA Modules:
  0.0 131.1 jit_solution(16378912057194327278)
XLA Ops:
  0.6 128.2 %shard_map.183 = (f32[16,8192]{1,0:T(8,128)}, f32[16,8192]{1,0:T(8,128)}, f32[64,128]{1,0:T(8,128)}, f32[1,128]{1,0:T(1,128)}) custom-call(f32[16,8192]{1,0:T(8,128)} %bitcast.8, f32[16,8192]{1,0:T(8,128)} %table.1, f32[16,8192]{1,0:T(8,128)} %hot.1, f32[64,128]{1,0:T(8,128)} %bitcast.9, s32[16,128]{1,0:T(8,128)} %bitcast.10, s32[16,128]{1,0:T(8,128)} %bitcast.11, ...), custom_call_target="tpu_custom_call" | custom-call | tf_op jit(solution)/shard_map/pallas_call | solution.py:626
  128.9 2.2 %shard_map.184 = (f32[16,8192]{1,0:T(8,128)}, f32[16,8192]{1,0:T(8,128)}, f32[64,128]{1,0:T(8,128)}, f32[1,128]{1,0:T(1,128)}) custom-call(f32[16,8192]{1,0:T(8,128)} %get-tuple-element.12.refs_0_, f32[16,8192]{1,0:T(8,128)} %get-tuple-element.13.refs_1_, f32[64,128]{1,0:T(8,128)} %get-tuple-element.14.refs_2_, f32[1,128]{1,0:T(1,128)} %get-tuple-element.15.refs_3_), custom_call_target="tpu_custom_call" | custom-call | tf_op jit(solution)/shard_map/pallas_call | solution.py:702

commit v4 on v3

--- a/solution.py
+++ b/solution.py
@@ -357,13 +357,13 @@
     def look(first, out):
         acc = None
         for p in range(8):
-            some = counts[pl.ds(pl.multiple_of(first, 256), 256), p * 512 : (p + 1) * 512]
+            some = counts[pl.ds(pl.multiple_of(first, 512), 512), p * 512 : (p + 1) * 512]
             for k in range(2):
                 term = lax.dot_general(
                     some, wide[k, p].reshape(256, 512), NT, preferred_element_type=F32
                 )
                 acc = term if acc is None else acc + term
-        out[...] = acc
+        out[...] = acc.reshape(2, 256, 256)
 
     renew(0, 8)
     encode()
@@ -382,16 +382,16 @@
 
     k_pool = []
 
-    @pl.loop(0, 4)
+    @pl.loop(0, 2)
     def _(m):
-        look(1024 + m * 256, for_twin.at[m])
+        look(1024 + m * 512, for_twin.at[pl.ds(m * 2, 2)])
 
     for m in range(4):
         k_pool.append(go(for_twin.at[m], pooled_in.at[m], twin))
 
-    @pl.loop(0, 4)
+    @pl.loop(0, 2)
     def _(m):
-        look(m * 256, pooled.at[m])
+        look(m * 512, pooled.at[pl.ds(m * 2, 2)])
 
     for m in range(4):
         landed(k_pool[m], pooled_in.at[m])

time: 131 us -> 130 us (level)
  no operation moved by 1% of the time
where the time goes in v4:
time: 130 us
  Pallas kernels  130 us (100%)
    pallas_call x1, Pallas kernels, step(): pl.pallas_call(step_kernel, out_shape=[jax.ShapeDtypeStruct((16, 8192), F...  127 us

profile of v4, /device:TPU:1, one launch (start us, length us, event | category | flops | bytes accessed | tf_op | source)
XLA Modules:
  0.0 130.2 jit_solution(4507151135140426368)
XLA Ops:
  0.6 127.4 %shard_map.183 = (f32[16,8192]{1,0:T(8,128)}, f32[16,8192]{1,0:T(8,128)}, f32[64,128]{1,0:T(8,128)}, f32[1,128]{1,0:T(1,128)}) custom-call(f32[16,8192]{1,0:T(8,128)} %bitcast.8, f32[16,8192]{1,0:T(8,128)} %table.1, f32[16,8192]{1,0:T(8,128)} %hot.1, f32[64,128]{1,0:T(8,128)} %bitcast.9, s32[16,128]{1,0:T(8,128)} %bitcast.10, s32[16,128]{1,0:T(8,128)} %bitcast.11, ...), custom_call_target="tpu_custom_call" | custom-call | tf_op jit(solution)/shard_map/pallas_call | solution.py:626
  128.0 2.2 %shard_map.184 = (f32[16,8192]{1,0:T(8,128)}, f32[16,8192]{1,0:T(8,128)}, f32[64,128]{1,0:T(8,128)}, f32[1,128]{1,0:T(1,128)}) custom-call(f32[16,8192]{1,0:T(8,128)} %get-tuple-element.12.refs_0_, f32[16,8192]{1,0:T(8,128)} %get-tuple-element.13.refs_1_, f32[64,128]{1,0:T(8,128)} %get-tuple-element.14.refs_2_, f32[1,128]{1,0:T(1,128)} %get-tuple-element.15.refs_3_), custom_call_target="tpu_custom_call" | custom-call | tf_op jit(solution)/shard_map/pallas_call | solution.py:702
